TPU v7x, 128 devices: a whole 4x4x4 slice. The times are simulated.
128 devices in a mesh: row: 8 (over y, x_lo), col: 16 (over z, x_hi, core).
Axes of the slice: x: 4 (x_hi: 2, x_lo: 2; x = x_hi * 2 + x_lo), y: 4, z: 4, core: 2. Of those that a mesh axis runs over, the one named last changes fastest.
Arguments:
- tokens: bfloat16 [16384, 3584], P(('row', 'col')), may hold values from -6 to 6
- expert_ids: int32 [16384, 4], P(('row', 'col')), may hold values from 0 to 127, all different within a row; in each aligned block of 128 rows (0 to 127, 128 to 255, ...) at most 5 rows name the same one
- combine_weights: float32 [16384, 4], P(('row', 'col')), may hold values from 0.1 to 1
- expert_gate: bfloat16 [128, 3584, 1024], P(('row', 'col')), may hold values from -0.09375 to 0.09375
- expert_up: bfloat16 [128, 3584, 1024], P(('row', 'col')), may hold values from -0.09375 to 0.09375
- expert_down: bfloat16 [128, 1024, 3584], P(('row', 'col')), may hold values from -0.1875 to 0.1875
- shared_gate: bfloat16 [3584, 1024], P(None, 'row'), may hold values from -0.09375 to 0.09375
- shared_up: bfloat16 [3584, 1024], P(None, 'row'), may hold values from -0.09375 to 0.09375
- shared_down: bfloat16 [1024, 3584], P('row'), may hold values from -0.1875 to 0.1875
Outputs:
- mixed: bfloat16 [16384, 3584], P(('row', 'col'))
Inputs may be any that keep to these rules, and one draw needn't show every extreme that they name: `expert_ids`: each row names 4 different experts. Among the 128 rows of one device no expert is named by more than 5 rows, and in every draw some expert is named by exactly 5 rows of some device.
All inputs are finite; a program needn't handle non-finite values.
Results may differ from a plain program's by a relative error of at most 0.0055.
Values may be sent and summed in bfloat16 or wider, within the bound.
A program may use at most 128 MiB of HBM per device.

v0:
```python
import jax
import jax.numpy as jnp
from jax import lax
from jax.sharding import Mesh
from jax.sharding import PartitionSpec as P

ROW = ("row_0", "row_1")
ROW_COL = ("row_0", "row_1", "col")


def own_rows(running, axes):
    for axis in axes:
        running = lax.psum_scatter(running, axis, scatter_dimension=0, tiled=True)
    return running


def expert_mlp(token_rows, gate_w, up_w, down_w):
    gate_proj = jnp.dot(token_rows, gate_w, preferred_element_type=jnp.float32)
    up_proj = jnp.dot(token_rows, up_w, preferred_element_type=jnp.float32)
    hidden = (jax.nn.silu(gate_proj) * up_proj).astype(jnp.bfloat16)
    return jnp.dot(hidden, down_w, preferred_element_type=jnp.float32).astype(jnp.bfloat16)


def place_slots(choices, experts, capacity):
    flat_ids = choices.reshape(-1)
    onehot = (flat_ids[:, None] == jnp.arange(experts, dtype=jnp.int32)[None, :]).astype(jnp.int32)
    running = jnp.cumsum(onehot, axis=0)
    slot_rank = jnp.sum(onehot * running, axis=1) - 1
    return flat_ids * capacity + slot_rank


def per_device(
    tokens,
    expert_ids,
    combine_weights,
    expert_gate,
    expert_up,
    expert_down,
    shared_gate,
    shared_up,
    shared_down,
):
    rows_here, model_width = tokens.shape
    choices_each = expert_ids.shape[1]
    row_devices = lax.axis_size(ROW)
    col_devices = lax.axis_size("col")
    experts = row_devices * col_devices
    capacity = max(2, 5 * rows_here * choices_each // (4 * experts))
    target = place_slots(expert_ids, experts, capacity)
    owner_row = jnp.arange(rows_here * choices_each, dtype=jnp.int32) // choices_each
    source_table = jnp.full((experts * capacity,), -1, jnp.int32).at[target].set(owner_row)
    filled = source_table >= 0
    outgoing = jnp.where(
        filled[:, None], tokens[jnp.maximum(source_table, 0)], jnp.zeros((), jnp.bfloat16)
    )
    arrived = lax.all_to_all(
        outgoing.reshape(experts, capacity, model_width),
        ROW_COL,
        split_axis=0,
        concat_axis=0,
        tiled=True,
    )
    results = expert_mlp(
        arrived.reshape(-1, model_width), expert_gate[0], expert_up[0], expert_down[0]
    )
    returned = lax.all_to_all(
        results.reshape(experts, capacity, model_width),
        ROW_COL,
        split_axis=0,
        concat_axis=0,
        tiled=True,
    )
    returned = returned.reshape(-1, model_width)
    picked = returned[target].reshape(rows_here, choices_each, model_width)
    routed = jnp.sum(picked.astype(jnp.float32) * combine_weights[:, :, None], axis=1)
    shard_rows = lax.all_gather(tokens, ROW, axis=0, tiled=True)
    gate_proj = jnp.dot(shard_rows, shared_gate, preferred_element_type=jnp.float32)
    up_proj = jnp.dot(shard_rows, shared_up, preferred_element_type=jnp.float32)
    shared_hidden = (jax.nn.silu(gate_proj) * up_proj).astype(jnp.bfloat16)
    shared = own_rows(jnp.dot(shared_hidden, shared_down, preferred_element_type=jnp.float32), ROW)
    return (routed + shared).astype(jnp.bfloat16)


def solution(mesh):
    finer = Mesh(mesh.devices.reshape(4, 2, mesh.shape["col"]), ("row_0", "row_1", "col"))
    placed = (
        P(ROW_COL, None),
        P(ROW_COL, None),
        P(ROW_COL, None),
        P(ROW_COL, None, None),
        P(ROW_COL, None, None),
        P(ROW_COL, None, None),
        P(None, ROW),
        P(None, ROW),
        P(ROW, None),
    )
    return jax.shard_map(
        per_device, mesh=finer, in_specs=placed, out_specs=P(ROW_COL, None), check_vma=False
    )
```

profile of v0, /device:TPU:32, one launch (start us, length us, event | category | flops | bytes accessed | tf_op | source)
XLA Modules:
  0.0 588.3 jit_solution(16821377509099226746)
XLA Ops:
  6.5 0.7 all-gather.2.cloned.1.call-update
  7.3 152.4 %all-gather.2.cloned.1.call-done = bf16[1024,3584]{1,0:T(8,128)(2,1)} async-done(((bf16[128,3584]{1,0:T(8,128)(2,1)}), bf16[1024,3584]{1,0:T(8,128)(2,1)}) %all-gather.2.cloned.1.call-update) | async-done | bytes 7340048 | tf_op jit(solution)/shard_map/all_gather | solution.py:76
  159.7 5.3 fusion.33
  165.1 15.9 %fusion.15 = f32[1024,3584]{1,0:T(8,128)} fusion(bf16[128,3584]{1,0:T(8,128)(2,1)S(1)} %copy-done, bf16[1024,3584]{1,0:T(8,128)(2,1)} %all-gather.2.cloned.1.call-done, bf16[3584,128]{1,0:T(8,128)(2,1)S(1)} %copy-done.3, f32[1024,128]{1,0:T(8,128)S(1)} %fusion.33), kind=kOutput, calls=%fused_computation.17 | convolution fusion | flops 1879834624 | bytes 24379392 | tf_op jit(solution)/shard_map/dot_general | solution.py:80
  181.1 0.6 copy-done.4
  181.7 0.1 copy.12
  181.8 0.1 eq.29
  181.9 0.1 eq.25
  182.0 0.1 copy.11
  182.1 0.1 mul.43
  182.2 0.1 copy.14
  182.3 0.2 fusion.23
  182.7 0.2 fusion.21
  182.9 2.4 scatter_custom_fusion
  185.4 0.2 broadcast_in_dim.26
  185.7 5.2 gather_fusion
  190.9 8.1 %gather.9 = bf16[128,5,3584]{2,1,0:T(8,128)(2,1)} reshape(bf16[640,3584]{1,0:T(8,128)(2,1)} %gather_fusion) | data formatting | bytes 9175040 | tf_op jit(solution)/shard_map/gather | solution.py:54
  198.9 4.0 broadcast_select_fusion
  202.9 111.2 %all_to_all.10 = bf16[128,5,3584]{2,1,0:T(8,128)(2,1)} all-to-all(bf16[128,5,3584]{2,1,0:T(8,128)(2,1)S(1)} %broadcast_select_fusion), channel_id=1, replica_groups=mesh['row_0'=4,'row_1'=2,'col'=16] {'row_0','row_1','col'}, dimensions={0} | all-to-all | bytes 9175040 | tf_op jit(solution)/shard_map/all_to_all | solution.py:56
  314.1 8.3 %reshape.73 = bf16[640,3584]{1,0:T(8,128)(2,1)} reshape(bf16[128,5,3584]{2,1,0:T(8,128)(2,1)} %all_to_all.10) | data formatting | bytes 9175040 | tf_op jit(solution)/shard_map/reshape | solution.py:64
  322.4 69.8 %reduce-scatter.3.cloned.1.call-done = f32[256,3584]{1,0:T(8,128)} async-done(((f32[1024,3584]{1,0:T(8,128)}), f32[256,3584]{1,0:T(8,128)}) %reduce-scatter.3.cloned.1.call-update) | async-done | bytes 3670032 | tf_op jit(solution)/shard_map/reduce_scatter | solution.py:13
  392.3 10.9 %fusion.4 = f32[640,1024]{1,0:T(8,128)} fusion(bf16[640,3584]{1,0:T(8,128)(2,1)} %reshape.73, bf16[1,3584,1024]{2,1,0:T(8,128)(2,1)} %param.12), kind=kOutput, calls=%fused_computation.7 | convolution fusion | flops 4697620480 | bytes 14548992 | tf_op jit(solution)/shard_map/dot_general | solution.py:18
  403.2 18.8 %fusion.6 = bf16[640,3584]{1,0:T(8,128)(2,1)} fusion(bf16[1,1024,3584]{2,1,0:T(8,128)(2,1)} %param.14, f32[640,1024]{1,0:T(8,128)} %fusion.4, bf16[640,3584]{1,0:T(8,128)(2,1)} %reshape.73, bf16[1,3584,1024]{2,1,0:T(8,128)(2,1)} %param.13), kind=kOutput, calls=%fused_computation.11 | convolution fusion | flops 9401466880 | bytes 26476544 | tf_op jit(solution)/shard_map/dot_general | solution.py:21
  422.0 7.8 %reshape.74 = bf16[128,5,3584]{2,1,0:T(8,128)(2,1)} reshape(bf16[640,3584]{1,0:T(8,128)(2,1)} %fusion.6) | data formatting | bytes 9175040 | tf_op jit(solution)/shard_map/reshape | solution.py:67
  429.8 11.8 %all-to-all-start.1 = ((bf16[128,5,3584]{2,1,0:T(8,128)(2,1)}), bf16[128,5,3584]{2,1,0:T(8,128)(2,1)}, u32[]{:S(2)}, u32[]{:S(2)}) async-start(bf16[128,5,3584]{2,1,0:T(8,128)(2,1)} %reshape.74), calls=%async_computation.1 | async-start | bytes 14680064 | tf_op jit(solution)/shard_map/all_to_all | solution.py:66
  441.7 0.1 copy.16
  441.8 102.7 %all-to-all-done.1 = bf16[128,5,3584]{2,1,0:T(8,128)(2,1)} async-done(((bf16[128,5,3584]{2,1,0:T(8,128)(2,1)}), bf16[128,5,3584]{2,1,0:T(8,128)(2,1)}, u32[]{:S(2)}, u32[]{:S(2)}) %all-to-all-start.1) | async-done | bytes 4587552 | tf_op jit(solution)/shard_map/all_to_all | solution.py:66
  544.4 8.1 %reshape.75 = bf16[640,3584]{1,0:T(8,128)(2,1)} reshape(bf16[128,5,3584]{2,1,0:T(8,128)(2,1)} %all-to-all-done.1) | data formatting | bytes 9175040 | tf_op jit(solution)/shard_map/reshape | solution.py:73
  552.6 10.8 %gather_fusion.1 = bf16[512,3584]{1,0:T(8,128)(2,1)} fusion(bf16[640,3584]{1,0:T(8,128)(2,1)} %reshape.75, s32[1024]{0:T(1024)S(1)} %pad_clamp_fusion), kind=kCustom, calls=%fused_computation.1 | custom fusion | bytes 7342080 | tf_op jit(solution)/shard_map/gather | solution.py:74
  563.4 7.5 %reshape.76 = f32[128,4,3584]{2,1,0:T(4,128)} reshape(bf16[512,3584]{1,0:T(8,128)(2,1)} %gather_fusion.1) | data formatting | bytes 11010048 | tf_op jit(solution)/shard_map/convert_element_type | solution.py:75
  570.9 8.3 %multiply_reduce_fusion = f32[128,3584]{1,0:T(8,128)S(1)} fusion(f32[128,4,3584]{2,1,0:T(4,128)} %reshape.76, f32[128,4]{1,0:T(8,128)S(1)} %copy.16), kind=kLoop, calls=%fused_computation.9 | loop fusion | flops 3211264 | bytes 9177088 | tf_op jit(solution)/shard_map/reduce_sum | solution.py:75
  579.2 2.6 add_convert_fusion
  (31 shorter events, 0.3 us)
Async XLA Ops:
  6.5 158.5 %copy-start = (bf16[128,3584]{1,0:T(8,128)(2,1)S(1)}, bf16[128,3584]{1,0:T(8,128)(2,1)}, u32[]{:S(2)}) copy-start(bf16[128,3584]{1,0:T(8,128)(2,1)} %param.17) | copy-start | bytes 2752516
  6.5 153.2 %all-gather.2.cloned.1.call-start = ((), (), s32[]{:S(2)}) async-start(), calls=%async_computation.4 | async-start | bytes 8257536 | tf_op jit(solution)/shard_map/all_gather | solution.py:76
  7.3 157.8 %copy-start.3 = (bf16[3584,128]{1,0:T(8,128)(2,1)S(1)}, bf16[3584,128]{1,0:T(8,128)(2,1)}, u32[]{:S(2)}) copy-start(bf16[3584,128]{1,0:T(8,128)(2,1)} %param.16) | copy-start | bytes 2752516
  7.3 385.0 %reduce-scatter.3.cloned.1.call-start = ((), (), s32[]{:S(2)}) async-start(), calls=%async_computation.5 | async-start | bytes 18350080 | tf_op jit(solution)/shard_map/reduce_scatter | solution.py:13
  181.0 0.7 copy-start.4
  181.0 4.6 copy-start.2
  181.0 398.2 %reduce-scatter.5.cloned.1.call-start = ((), (), s32[]{:S(2)}) async-start(), calls=%async_computation.6 | async-start | bytes 5505024 | tf_op jit(solution)/shard_map/reduce_scatter | solution.py:13
  429.8 11.8 %copy-start.5 = (f32[128,4]{0,1:T(4,128)S(1)}, f32[128,4]{0,1:T(4,128)}, u32[]{:S(2)}) copy-start(f32[128,4]{0,1:T(4,128)} %param.11) | copy-start | bytes 6148
  429.8 114.6 %all-to-all-start.1 = ((bf16[128,5,3584]{2,1,0:T(8,128)(2,1)}), bf16[128,5,3584]{2,1,0:T(8,128)(2,1)}, u32[]{:S(2)}, u32[]{:S(2)}) async-start(bf16[128,5,3584]{2,1,0:T(8,128)(2,1)} %reshape.74), calls=%async_computation.1 | async-start | bytes 14680064 | tf_op jit(solution)/shard_map/all_to_all | solution.py:66
  570.9 10.9 %copy-start.1 = (bf16[128,3584]{1,0:T(8,128)(2,1)S(1)}, bf16[128,3584]{1,0:T(8,128)(2,1)}, u32[]{:S(2)}) copy-start(bf16[128,3584]{1,0:T(8,128)(2,1)} %param.17) | copy-start | bytes 2752516
Sparse Core Ops, SparseCore 0:
  9.0 150.6 all-gather.1
  181.1 211.1 reduce-scatter.2
  394.6 59.4 reduce-scatter.4
where the time goes:
time: 590 us; the launch traced here: 588 us
  waiting for transfers between devices  326 us (55%)
  blocking collectives  111 us (19%)
  local copies, waits for them, and re-layouts  60 us (10%)
  matrix products  50.9 us (9%)
  other arithmetic  15.4 us (3%)
  between operations  13.3 us (2%)
  starting transfers between devices  11.9 us (2%)
    all_gather x1, waiting for transfers between devices, per_device(): shard_rows = lax.all_gather(tokens, ROW, axis=0, tiled=True)  152 us
    all_to_all x1, blocking collectives, per_device(): lax.all_to_all(outgoing.reshape(experts, capacity, model_width), ROW_COL,...  111 us
    all_to_all x1, waiting for transfers between devices, per_device(): lax.all_to_all(results.reshape(experts, capacity, model_width), ROW_COL,...  103 us
    reduce_scatter x2, waiting for transfers between devices, own_rows(): running = lax.psum_scatter(running, axis, scatter_dimension=0, tiled=True)  69.9 us
    dot_general x1, matrix products, expert_mlp(): jnp.dot(hidden, down_w, preferred_element_type=jnp.float32)  18.8 us
    dot_general x1, matrix products, per_device(): jnp.dot(shared_hidden, shared_down, preferred_element_type=jnp.float32)  15.9 us
    gather x2, local copies, waits for them, and re-layouts, per_device(): tokens[jnp.maximum(source_table, 0)]  13.3 us
    all_to_all x1, starting transfers between devices, per_device(): lax.all_to_all(results.reshape(experts, capacity, model_width), ROW_COL,...  11.8 us
  transfers between devices with their start and end apart: 4, of which 3 were waited for; matrix products, arithmetic and copies ran while one was open for 17% of the time, Pallas kernels for 0%

commit v1 on v0

--- a/solution.py
+++ b/solution.py
@@ -6,6 +6,15 @@
 
 ROW = ("row_0", "row_1")
 ROW_COL = ("row_0", "row_1", "col")
+
+
+def turn_racks(piece_in):
+    return jnp.concatenate(
+        lax.all_to_all(
+            jnp.stack([piece_in] * lax.axis_size(ROW)), axis_name=ROW, split_axis=0, concat_axis=0
+        ),
+        axis=0,
+    )
 
 
 def own_rows(running, axes):
@@ -73,7 +82,7 @@
     returned = returned.reshape(-1, model_width)
     picked = returned[target].reshape(rows_here, choices_each, model_width)
     routed = jnp.sum(picked.astype(jnp.float32) * combine_weights[:, :, None], axis=1)
-    shard_rows = lax.all_gather(tokens, ROW, axis=0, tiled=True)
+    shard_rows = turn_racks(tokens)
     gate_proj = jnp.dot(shard_rows, shared_gate, preferred_element_type=jnp.float32)
     up_proj = jnp.dot(shard_rows, shared_up, preferred_element_type=jnp.float32)
     shared_hidden = (jax.nn.silu(gate_proj) * up_proj).astype(jnp.bfloat16)

time: 590 us -> 528 us (0.89)
  waiting for transfers between devices: 326 us -> 174 us
  blocking collectives: 111 us -> 200 us
    all_gather x1 -> x0, waiting for transfers between devices: 152 us -> none  [per_device(): shard_rows = lax.all_gather(tokens, ROW, axis=0, tiled=True)]
    all_to_all x0 -> x1, blocking collectives: none -> 89.6 us  [turn_racks(): lax.all_to_all(jnp.stack([piece_in] * lax.axis_size(ROW)), axis_name=ROW,...]
  transfers between devices with their start and end apart: 4 -> 3, of which waited for: 3 -> 2; matrix products, arithmetic and copies ran while one was open for 17% -> 19% of each run, Pallas kernels for 0% -> 0%
where the time goes in v1:
time: 528 us; the launch traced here: 526 us
  blocking collectives  200 us (38%)
  waiting for transfers between devices  174 us (33%)
  local copies, waits for them, and re-layouts  64.6 us (12%)
  matrix products  47.6 us (9%)
  other arithmetic  15.3 us (3%)
  between operations  13.6 us (3%)
  starting transfers between devices  11.8 us (2%)
    all_to_all x1, blocking collectives, per_device(): lax.all_to_all(outgoing.reshape(experts, capacity, model_width), ROW_COL,...  110 us
    all_to_all x1, waiting for transfers between devices, per_device(): lax.all_to_all(results.reshape(experts, capacity, model_width), ROW_COL,...  104 us
    all_to_all x1, blocking collectives, turn_racks(): lax.all_to_all(jnp.stack([piece_in] * lax.axis_size(ROW)), axis_name=ROW,...  89.6 us
    reduce_scatter x2, waiting for transfers between devices, own_rows(): running = lax.psum_scatter(running, axis, scatter_dimension=0, tiled=True)  69.9 us
    dot_general x1, matrix products, expert_mlp(): jnp.dot(hidden, down_w, preferred_element_type=jnp.float32)  18.8 us
    dot_general x1, matrix products, per_device(): jnp.dot(shared_hidden, shared_down, preferred_element_type=jnp.float32)  15.9 us
    gather x2, local copies, waits for them, and re-layouts, per_device(): tokens[jnp.maximum(source_table, 0)]  13.1 us
    all_to_all x1, starting transfers between devices, per_device(): lax.all_to_all(results.reshape(experts, capacity, model_width), ROW_COL,...  11.8 us
  transfers between devices with their start and end apart: 3, of which 2 were waited for; matrix products, arithmetic and copies ran while one was open for 19% of the time, Pallas kernels for 0%

profile of v1, /device:TPU:32, one launch (start us, length us, event | category | flops | bytes accessed | tf_op | source)
XLA Modules:
  0.0 526.4 jit_solution(11594685543665104018)
XLA Ops:
  6.5 1.9 stack.2
  8.4 89.6 %all_to_all.15 = bf16[8,128,3584]{2,1,0:T(8,128)(2,1)S(1)} all-to-all(bf16[8,128,3584]{2,1,0:T(8,128)(2,1)S(1)} %stack.2), channel_id=1, replica_groups=mesh['row_0'=4,'row_1'=2,'col'=16] {'row_0','row_1'}, dimensions={0} | all-to-all | bytes 14680064 | tf_op jit(solution)/shard_map/all_to_all | solution.py:13
  98.1 2.9 copy-done.3
  101.0 2.1 fusion.33
  103.1 15.9 %fusion.15 = f32[1024,3584]{1,0:T(8,128)} fusion(bf16[128,3584]{1,0:T(8,128)(2,1)S(1)} %copy-done, bf16[1024,3584]{1,0:T(8,128)(2,1)} %bitcast.38, bf16[3584,128]{1,0:T(8,128)(2,1)S(1)} %copy-done.4, f32[1024,128]{1,0:T(8,128)S(1)} %fusion.33), kind=kOutput, calls=%fused_computation.17 | convolution fusion | flops 1879834624 | bytes 24379392 | tf_op jit(solution)/shard_map/dot_general | solution.py:89
  119.1 0.6 copy-done.5
  119.7 0.1 copy.12
  119.9 0.1 eq.25
  120.0 0.1 copy.11
  120.1 0.1 mul.43
  120.2 0.1 copy.14
  120.3 0.2 fusion.23
  120.7 0.2 fusion.21
  120.9 2.4 scatter_custom_fusion
  123.4 0.2 broadcast_in_dim.26
  123.7 5.2 gather_fusion
  128.9 7.9 %gather.9 = bf16[128,5,3584]{2,1,0:T(8,128)(2,1)} reshape(bf16[640,3584]{1,0:T(8,128)(2,1)} %gather_fusion) | data formatting | bytes 9175040 | tf_op jit(solution)/shard_map/gather | solution.py:63
  136.8 3.9 broadcast_select_fusion
  140.7 110.0 %all_to_all.16 = bf16[128,5,3584]{2,1,0:T(8,128)(2,1)} all-to-all(bf16[128,5,3584]{2,1,0:T(8,128)(2,1)S(1)} %broadcast_select_fusion), channel_id=1, replica_groups=mesh['row_0'=4,'row_1'=2,'col'=16] {'row_0','row_1','col'}, dimensions={0} | all-to-all | bytes 9175040 | tf_op jit(solution)/shard_map/all_to_all | solution.py:65
  250.7 8.3 %reshape.78 = bf16[640,3584]{1,0:T(8,128)(2,1)} reshape(bf16[128,5,3584]{2,1,0:T(8,128)(2,1)} %all_to_all.16) | data formatting | bytes 9175040 | tf_op jit(solution)/shard_map/reshape | solution.py:73
  259.1 69.9 %reduce-scatter.3.cloned.1.call-done = f32[256,3584]{1,0:T(8,128)} async-done(((f32[1024,3584]{1,0:T(8,128)}), f32[256,3584]{1,0:T(8,128)}) %reduce-scatter.3.cloned.1.call-update) | async-done | bytes 3670032 | tf_op jit(solution)/shard_map/reduce_scatter | solution.py:22
  329.0 10.9 %fusion.4 = f32[640,1024]{1,0:T(8,128)} fusion(bf16[640,3584]{1,0:T(8,128)(2,1)} %reshape.78, bf16[1,3584,1024]{2,1,0:T(8,128)(2,1)} %param.12), kind=kOutput, calls=%fused_computation.7 | convolution fusion | flops 4697620480 | bytes 14548992 | tf_op jit(solution)/shard_map/dot_general | solution.py:27
  339.9 18.8 %fusion.6 = bf16[640,3584]{1,0:T(8,128)(2,1)} fusion(bf16[1,1024,3584]{2,1,0:T(8,128)(2,1)} %param.14, f32[640,1024]{1,0:T(8,128)} %fusion.4, bf16[640,3584]{1,0:T(8,128)(2,1)} %reshape.78, bf16[1,3584,1024]{2,1,0:T(8,128)(2,1)} %param.13), kind=kOutput, calls=%fused_computation.11 | convolution fusion | flops 9401466880 | bytes 26476544 | tf_op jit(solution)/shard_map/dot_general | solution.py:30
  358.7 7.8 %reshape.79 = bf16[128,5,3584]{2,1,0:T(8,128)(2,1)} reshape(bf16[640,3584]{1,0:T(8,128)(2,1)} %fusion.6) | data formatting | bytes 9175040 | tf_op jit(solution)/shard_map/reshape | solution.py:76
  366.5 11.8 %all-to-all-start.1 = ((bf16[128,5,3584]{2,1,0:T(8,128)(2,1)}), bf16[128,5,3584]{2,1,0:T(8,128)(2,1)}, u32[]{:S(2)}, u32[]{:S(2)}) async-start(bf16[128,5,3584]{2,1,0:T(8,128)(2,1)} %reshape.79), calls=%async_computation.1 | async-start | bytes 14680064 | tf_op jit(solution)/shard_map/all_to_all | solution.py:75
  378.3 0.1 copy.16
  378.5 103.8 %all-to-all-done.1 = bf16[128,5,3584]{2,1,0:T(8,128)(2,1)} async-done(((bf16[128,5,3584]{2,1,0:T(8,128)(2,1)}), bf16[128,5,3584]{2,1,0:T(8,128)(2,1)}, u32[]{:S(2)}, u32[]{:S(2)}) %all-to-all-start.1) | async-done | bytes 4587552 | tf_op jit(solution)/shard_map/all_to_all | solution.py:75
  482.2 8.1 %reshape.80 = bf16[640,3584]{1,0:T(8,128)(2,1)} reshape(bf16[128,5,3584]{2,1,0:T(8,128)(2,1)} %all-to-all-done.1) | data formatting | bytes 9175040 | tf_op jit(solution)/shard_map/reshape | solution.py:82
  490.4 10.8 %gather_fusion.1 = bf16[512,3584]{1,0:T(8,128)(2,1)} fusion(bf16[640,3584]{1,0:T(8,128)(2,1)} %reshape.80, s32[1024]{0:T(1024)S(1)} %pad_clamp_fusion), kind=kCustom, calls=%fused_computation.1 | custom fusion | bytes 7342080 | tf_op jit(solution)/shard_map/gather | solution.py:83
  501.2 7.5 %reshape.82 = f32[128,4,3584]{2,1,0:T(4,128)} reshape(bf16[512,3584]{1,0:T(8,128)(2,1)} %gather_fusion.1) | data formatting | bytes 11010048 | tf_op jit(solution)/shard_map/convert_element_type | solution.py:84
  508.7 8.3 %multiply_reduce_fusion = f32[128,3584]{1,0:T(8,128)S(1)} fusion(f32[128,4,3584]{2,1,0:T(4,128)} %reshape.82, f32[128,4]{1,0:T(8,128)S(1)} %copy.16), kind=kLoop, calls=%fused_computation.9 | loop fusion | flops 3211264 | bytes 9177088 | tf_op jit(solution)/shard_map/reduce_sum | solution.py:84
  517.0 2.6 add_convert_fusion
  (34 shorter events, 0.4 us)
Async XLA Ops:
  6.5 96.5 %copy-start = (bf16[128,3584]{1,0:T(8,128)(2,1)S(1)}, bf16[128,3584]{1,0:T(8,128)(2,1)}, u32[]{:S(2)}) copy-start(bf16[128,3584]{1,0:T(8,128)(2,1)} %param.17) | copy-start | bytes 2752516
  6.5 322.4 %reduce-scatter.3.cloned.1.call-start = ((), (), s32[]{:S(2)}) async-start(), calls=%async_computation.5 | async-start | bytes 18350080 | tf_op jit(solution)/shard_map/reduce_scatter | solution.py:22
  8.4 92.6 %copy-start.7 = (bf16[3584,128]{1,0:T(8,128)(2,1)S(1)}, bf16[3584,128]{1,0:T(8,128)(2,1)}, u32[]{:S(2)}) copy-start(bf16[3584,128]{1,0:T(8,128)(2,1)} %param.15) | copy-start | bytes 2752516
  98.1 2.9 copy-start.3
  101.0 2.1 copy-start.4
  119.0 0.7 copy-start.5
  119.0 4.6 copy-start.2
  119.0 398.0 %reduce-scatter.5.cloned.1.call-start = ((), (), s32[]{:S(2)}) async-start(), calls=%async_computation.6 | async-start | bytes 5505024 | tf_op jit(solution)/shard_map/reduce_scatter | solution.py:22
  366.5 11.8 %copy-start.6 = (f32[128,4]{0,1:T(4,128)S(1)}, f32[128,4]{0,1:T(4,128)}, u32[]{:S(2)}) copy-start(f32[128,4]{0,1:T(4,128)} %param.11) | copy-start | bytes 6148
  366.5 115.7 %all-to-all-start.1 = ((bf16[128,5,3584]{2,1,0:T(8,128)(2,1)}), bf16[128,5,3584]{2,1,0:T(8,128)(2,1)}, u32[]{:S(2)}, u32[]{:S(2)}) async-start(bf16[128,5,3584]{2,1,0:T(8,128)(2,1)} %reshape.79), calls=%async_computation.1 | async-start | bytes 14680064 | tf_op jit(solution)/shard_map/all_to_all | solution.py:75
  508.7 10.9 %copy-start.1 = (bf16[128,3584]{1,0:T(8,128)(2,1)S(1)}, bf16[128,3584]{1,0:T(8,128)(2,1)}, u32[]{:S(2)}) copy-start(bf16[128,3584]{1,0:T(8,128)(2,1)} %param.17) | copy-start | bytes 2752516
Sparse Core Ops, SparseCore 0:
  119.1 209.7 reduce-scatter.2
  331.3 59.4 reduce-scatter.4
